TPU v7x, 512 devices: a whole 4x8x8 slice. The times are simulated.
512 devices in a mesh: seq: 64 (over z_lo, y, core), head: 8 (over z_hi, x).
Axes of the slice: x: 4, y: 8, z: 8 (z_hi: 2, z_lo: 4; z = z_hi * 4 + z_lo), core: 2. Of those that a mesh axis runs over, the one named last changes fastest.
Arguments:
- queries: bfloat16 [8192, 64, 128], P('seq', 'head'), may hold values from -11 to 11
- key_heads: bfloat16 [8192, 8, 128], P('seq', 'head'), may hold values from -20 to 20
- value_heads: bfloat16 [8192, 8, 128], P('seq', 'head'), may hold values from -6 to 6
- fold_map: int32 [64], replicated, may hold values from 0 to 63, as said below
- partner_map: int32 [2, 64], replicated, may hold values from 0 to 63, as said below
- out_weight: bfloat16 [8192, 5120], P('head', 'seq'), may hold values from -0.1875 to 0.1875
Outputs:
- projected: bfloat16 [8192, 5120], P('seq', 'head')
Inputs may be any that keep to these rules, and one draw needn't show every extreme that they name: `fold_map`: a permutation of 0 to 63. `partner_map`: round r pairs index i with index i XOR m_r, where m_r is nonzero and the two rounds have different m_r.
All inputs are finite; a program needn't handle non-finite values.
Results may differ from a plain program's by a relative error of at most 0.0051.
Values may be sent and summed in bfloat16 or wider, within the bound.
A program may use at most 64 MiB of HBM per device.

v0:
```python
import math
import jax
import jax.numpy as jnp
from jax import lax
from jax.sharding import PartitionSpec as P


def from_partner(shard, axis, distance):
    return lax.ppermute(shard, axis, [(i, i ^ 1 << distance) for i in range(lax.axis_size(axis))])


def per_device(queries, key_heads, value_heads, fold_map, partner_map, out_weight):
    my_index = lax.axis_index("seq")
    seq_count = lax.axis_size("seq")
    half_rows = queries.shape[0] // 2
    all_rows = 2 * half_rows
    local_kv = key_heads.shape[1]
    group_size = queries.shape[1] // local_kv
    head_dim = queries.shape[2]
    score_scale = 1.0 / math.sqrt(head_dim)
    query_groups = queries.reshape(all_rows, local_kv, group_size, head_dim)
    offsets = jnp.arange(half_rows, dtype=jnp.int32)

    def places_of(device):
        lower_block = fold_map[device]
        return jnp.concatenate(
            [
                lower_block * half_rows + offsets,
                (2 * seq_count - 1 - lower_block) * half_rows + offsets,
            ]
        )

    def raw_scores(query_part, key_part):
        return (
            jnp.einsum("rhje,khe->hjrk", query_part, key_part, preferred_element_type=jnp.float32)
            * score_scale
        )

    def weighted_sum(weights, value_part):
        return jnp.einsum(
            "hjrk,khe->rhje",
            weights.astype(jnp.bfloat16),
            value_part,
            preferred_element_type=jnp.float32,
        )

    my_places = places_of(my_index)
    own_scores = jnp.where(
        my_places[None, :] <= my_places[:, None], raw_scores(query_groups, key_heads), -jnp.inf
    )
    partner_a = partner_map[0, my_index]
    partner_b = partner_map[1, my_index]
    flip_a = jnp.bitwise_xor(partner_a, my_index)
    flip_b = jnp.bitwise_xor(partner_b, my_index)
    bit_count = seq_count.bit_length() - 1
    own_pair = jnp.stack([key_heads, value_heads])

    def route_pair(flip_mask):
        moving = own_pair
        for bit_index in range(bit_count):
            arrived = from_partner(moving, "seq", bit_index)
            take_this = jnp.bitwise_and(jnp.right_shift(flip_mask, bit_index), 1) == 1
            moving = jnp.where(take_this, arrived, moving)
        return moving

    pair_a = route_pair(flip_a)
    pair_b = route_pair(flip_b)
    own_max = jnp.max(own_scores, axis=-1)
    remote = []
    row_max = own_max
    for partner, moved_pair in ((partner_a, pair_a), (partner_b, pair_b)):
        their_places = places_of(partner)
        scores = jnp.where(
            their_places[None, :] <= my_places[:, None],
            raw_scores(query_groups, moved_pair[0]),
            -jnp.inf,
        )
        row_max = jnp.maximum(row_max, jnp.max(scores, axis=-1))
        remote.append((scores, moved_pair[1]))
    own_weights = jnp.exp(own_scores - row_max[..., None])
    row_total = jnp.sum(own_weights, axis=-1)
    weighted = weighted_sum(own_weights, value_heads)
    for scores, value_part in remote:
        weights = jnp.exp(scores - row_max[..., None])
        row_total = row_total + jnp.sum(weights, axis=-1)
        weighted = weighted + weighted_sum(weights, value_part)
    attended = (weighted / jnp.moveaxis(row_total, 2, 0)[..., None]).astype(jnp.bfloat16)
    flat_rows = attended.reshape(all_rows, local_kv * group_size * head_dim)
    partial_terms = jnp.dot(
        flat_rows,
        lax.all_gather(out_weight, "seq", axis=1, tiled=True),
        preferred_element_type=jnp.float32,
    )
    return lax.psum_scatter(partial_terms, "head", scatter_dimension=1, tiled=True).astype(
        jnp.bfloat16
    )


def solution(mesh):
    return jax.shard_map(
        per_device,
        mesh=mesh,
        in_specs=(
            P("seq", "head", None),
            P("seq", "head", None),
            P("seq", "head", None),
            P(),
            P(),
            P("head", "seq"),
        ),
        out_specs=P("seq", "head"),
        check_vma=False,
    )
```

profile of v0, /device:TPU:8, one launch (start us, length us, event | category | flops | bytes accessed | tf_op | source)
XLA Modules:
  0.0 270.4 jit_solution(317472850337719558)
XLA Ops:
  6.5 0.7 all-gather.2.cloned.1.call-update
  7.3 0.8 pad_maximum_fusion
  8.1 1.9 collective-permute-start
  10.0 1.4 constant_dynamic-slice_fusion.1
  15.2 1.4 fusion.31
  21.8 0.8 broadcast_select_fusion.6
  22.6 7.7 %collective-permute-start.1 = (bf16[2,128,1,128]{3,1,2,0:T(8,128)(2,1)S(1)}, bf16[2,128,1,128]{3,1,2,0:T(8,128)(2,1)S(1)}, u32[]{:S(2)}, u32[]{:S(2)}) collective-permute-start(bf16[2,128,1,128]{3,1,2,0:T(8,128)(2,1)S(1)} %get-tuple-element.8), channel_id=1, source_target_pairs={{0,16},{8,24},{16,0},{24,8},{32,48},{40,56},{48,32},{56,40},{64,80... | collective-permute-start | bytes 196616 | tf_op jit(solution)/shard_map/ppermute | solution.py:9
  30.3 1.0 fusion.33
  31.4 1.9 collective-permute-start.6
  33.3 0.3 collective-permute-done.1
  33.6 1.9 collective-permute-start.2
  35.6 3.4 %collective-permute-done.6 = bf16[2,128,1,128]{3,1,2,0:T(8,128)(2,1)S(1)} collective-permute-done((bf16[2,128,1,128]{3,1,2,0:T(8,128)(2,1)S(1)}, bf16[2,128,1,128]{3,1,2,0:T(8,128)(2,1)S(1)}, u32[]{:S(2)}, u32[]{:S(2)}) %collective-permute-start.6) | collective-permute-done | bytes 65568 | tf_op jit(solution)/shard_map/ppermute | solution.py:9
  39.0 1.9 collective-permute-start.7
  40.9 1.1 collective-permute-done.2
  42.0 1.9 collective-permute-start.3
  44.0 2.9 %collective-permute-done.7 = bf16[2,128,1,128]{3,1,2,0:T(8,128)(2,1)S(1)} collective-permute-done((bf16[2,128,1,128]{3,1,2,0:T(8,128)(2,1)S(1)}, bf16[2,128,1,128]{3,1,2,0:T(8,128)(2,1)S(1)}, u32[]{:S(2)}, u32[]{:S(2)}) %collective-permute-start.7) | collective-permute-done | bytes 65568 | tf_op jit(solution)/shard_map/ppermute | solution.py:9
  46.9 5.0 %collective-permute-start.8 = (bf16[2,128,1,128]{3,1,2,0:T(8,128)(2,1)S(1)}, bf16[2,128,1,128]{3,1,2,0:T(8,128)(2,1)S(1)}, u32[]{:S(2)}, u32[]{:S(2)}) collective-permute-start(bf16[2,128,1,128]{3,1,2,0:T(8,128)(2,1)S(1)} %broadcast_select_fusion.2), channel_id=1, source_target_pairs={{0,64},{8,72},{16,80},{24,88},{32,96},{40,104},{48,112},{56,120},{... | collective-permute-start | bytes 196616 | tf_op jit(solution)/shard_map/ppermute | solution.py:9
  51.8 1.8 collective-permute-done.3
  53.6 1.9 collective-permute-start.4
  55.5 3.6 %collective-permute-done.8 = bf16[2,128,1,128]{3,1,2,0:T(8,128)(2,1)S(1)} collective-permute-done((bf16[2,128,1,128]{3,1,2,0:T(8,128)(2,1)S(1)}, bf16[2,128,1,128]{3,1,2,0:T(8,128)(2,1)S(1)}, u32[]{:S(2)}, u32[]{:S(2)}) %collective-permute-start.8) | collective-permute-done | bytes 65568 | tf_op jit(solution)/shard_map/ppermute | solution.py:9
  59.1 1.9 collective-permute-start.9
  61.1 6.5 %collective-permute-start.5 = (bf16[2,128,1,128]{3,1,2,0:T(8,128)(2,1)S(1)}, bf16[2,128,1,128]{3,1,2,0:T(8,128)(2,1)S(1)}, u32[]{:S(2)}, u32[]{:S(2)}) collective-permute-start(bf16[2,128,1,128]{3,1,2,0:T(8,128)(2,1)S(1)} %broadcast_select_fusion.10), channel_id=1, source_target_pairs={{0,256},{8,264},{16,272},{24,280},{32,288},{40,296},{48,304},{56,3... | collective-permute-start | bytes 196616 | tf_op jit(solution)/shard_map/ppermute | solution.py:9
  67.6 2.2 collective-permute-start.10
  69.7 3.3 %collective-permute-done.5 = bf16[2,128,1,128]{3,1,2,0:T(8,128)(2,1)S(1)} collective-permute-done((bf16[2,128,1,128]{3,1,2,0:T(8,128)(2,1)S(1)}, bf16[2,128,1,128]{3,1,2,0:T(8,128)(2,1)S(1)}, u32[]{:S(2)}, u32[]{:S(2)}) %collective-permute-start.5) | collective-permute-done | bytes 65568 | tf_op jit(solution)/shard_map/ppermute | solution.py:9
  73.1 3.0 %collective-permute-done.10 = bf16[2,128,1,128]{3,1,2,0:T(8,128)(2,1)S(1)} collective-permute-done((bf16[2,128,1,128]{3,1,2,0:T(8,128)(2,1)S(1)}, bf16[2,128,1,128]{3,1,2,0:T(8,128)(2,1)S(1)}, u32[]{:S(2)}, u32[]{:S(2)}) %collective-permute-start.10) | collective-permute-done | bytes 65568 | tf_op jit(solution)/shard_map/ppermute | solution.py:9
  76.9 0.2 fusion.17
  77.2 1.0 convolution_bitcast_fusion
  78.2 0.3 fusion.9
  78.5 66.9 %all-gather.2.cloned.1.call-done = bf16[1024,5120]{0,1:T(8,128)(2,1)} async-done(((bf16[1024,80]{0,1:T(8,128)(2,1)}), bf16[1024,5120]{0,1:T(8,128)(2,1)}) %all-gather.2.cloned.1.call-update) | async-done | bytes 10485776 | tf_op jit(solution)/shard_map/all_gather | solution.py:91
  145.4 9.1 %fusion.35 = f32[128,5120]{1,0:T(8,128)} fusion(bf16[128,1024]{0,1:T(8,128)(2,1)S(1)} %bitcast.95, bf16[1024,5120]{0,1:T(8,128)(2,1)} %all-gather.2.cloned.1.call-done), kind=kOutput, calls=%fused_computation.73 | convolution fusion | flops 1342177280 | bytes 13369344 | tf_op jit(solution)/shard_map/dot_general | solution.py:89
  154.5 107.4 %reduce-scatter.2.cloned.1.call-done = f32[128,640]{1,0:T(8,128)} async-done(((f32[128,5120]{1,0:T(8,128)}), f32[128,640]{1,0:T(8,128)}) %reduce-scatter.2.cloned.1.call-update) | async-done | bytes 327696 | tf_op jit(solution)/shard_map/reduce_scatter | solution.py:94
  261.9 1.7 convert_element_type.19
  (30 shorter events, 1.3 us)
Async XLA Ops:
  6.5 23.8 %copy-start = (bf16[128,8,128]{2,1,0:T(8,128)(2,1)S(1)}, bf16[128,8,128]{2,1,0:T(8,128)(2,1)}, u32[]{:S(2)}) copy-start(bf16[128,8,128]{2,1,0:T(8,128)(2,1)} %param.6) | copy-start | bytes 786436
  6.5 138.8 %all-gather.2.cloned.1.call-start = ((), (), s32[]{:S(2)}) async-start(), calls=%async_computation.1 | async-start | bytes 10649600 | tf_op jit(solution)/shard_map/all_gather | solution.py:91
  7.3 254.7 %reduce-scatter.2.cloned.1.call-start = ((), (), s32[]{:S(2)}) async-start(), calls=%async_computation.2 | async-start | bytes 2949120 | tf_op jit(solution)/shard_map/reduce_scatter | solution.py:94
  8.1 13.7 %collective-permute-start = (bf16[2,128,1,128]{3,1,2,0:T(8,128)(2,1)S(1)}, bf16[2,128,1,128]{3,1,2,0:T(8,128)(2,1)S(1)}, u32[]{:S(2)}, u32[]{:S(2)}) collective-permute-start(bf16[2,128,1,128]{3,1,2,0:T(8,128)(2,1)S(1)} %pad_maximum_fusion), channel_id=1, source_target_pairs={{0,8},{8,0},{16,24},{24,16},{32,40},{40,32},{48,56},{56,48},{64,72... | collective-permute-start | bytes 196616 | tf_op jit(solution)/shard_map/ppermute | solution.py:9
  22.6 11.0 %collective-permute-start.1 = (bf16[2,128,1,128]{3,1,2,0:T(8,128)(2,1)S(1)}, bf16[2,128,1,128]{3,1,2,0:T(8,128)(2,1)S(1)}, u32[]{:S(2)}, u32[]{:S(2)}) collective-permute-start(bf16[2,128,1,128]{3,1,2,0:T(8,128)(2,1)S(1)} %get-tuple-element.8), channel_id=1, source_target_pairs={{0,16},{8,24},{16,0},{24,8},{32,48},{40,56},{48,32},{56,40},{64,80... | collective-permute-start | bytes 196616 | tf_op jit(solution)/shard_map/ppermute | solution.py:9
  31.4 7.6 %collective-permute-start.6 = (bf16[2,128,1,128]{3,1,2,0:T(8,128)(2,1)S(1)}, bf16[2,128,1,128]{3,1,2,0:T(8,128)(2,1)S(1)}, u32[]{:S(2)}, u32[]{:S(2)}) collective-permute-start(bf16[2,128,1,128]{3,1,2,0:T(8,128)(2,1)S(1)} %get-tuple-element.9), channel_id=1, source_target_pairs={{0,16},{8,24},{16,0},{24,8},{32,48},{40,56},{48,32},{56,40},{64,80... | collective-permute-start | bytes 196616 | tf_op jit(solution)/shard_map/ppermute | solution.py:9
  33.6 8.4 %collective-permute-start.2 = (bf16[2,128,1,128]{3,1,2,0:T(8,128)(2,1)S(1)}, bf16[2,128,1,128]{3,1,2,0:T(8,128)(2,1)S(1)}, u32[]{:S(2)}, u32[]{:S(2)}) collective-permute-start(bf16[2,128,1,128]{3,1,2,0:T(8,128)(2,1)S(1)} %broadcast_select_fusion.7), channel_id=1, source_target_pairs={{0,32},{8,40},{16,48},{24,56},{32,0},{40,8},{48,16},{56,24},{64,96... | collective-permute-start | bytes 196616 | tf_op jit(solution)/shard_map/ppermute | solution.py:9
  39.0 7.8 %collective-permute-start.7 = (bf16[2,128,1,128]{3,1,2,0:T(8,128)(2,1)S(1)}, bf16[2,128,1,128]{3,1,2,0:T(8,128)(2,1)S(1)}, u32[]{:S(2)}, u32[]{:S(2)}) collective-permute-start(bf16[2,128,1,128]{3,1,2,0:T(8,128)(2,1)S(1)} %broadcast_select_fusion.1), channel_id=1, source_target_pairs={{0,32},{8,40},{16,48},{24,56},{32,0},{40,8},{48,16},{56,24},{64,96... | collective-permute-start | bytes 196616 | tf_op jit(solution)/shard_map/ppermute | solution.py:9
  42.0 11.6 %collective-permute-start.3 = (bf16[2,128,1,128]{3,1,2,0:T(8,128)(2,1)S(1)}, bf16[2,128,1,128]{3,1,2,0:T(8,128)(2,1)S(1)}, u32[]{:S(2)}, u32[]{:S(2)}) collective-permute-start(bf16[2,128,1,128]{3,1,2,0:T(8,128)(2,1)S(1)} %broadcast_select_fusion.8), channel_id=1, source_target_pairs={{0,64},{8,72},{16,80},{24,88},{32,96},{40,104},{48,112},{56,120},{... | collective-permute-start | bytes 196616 | tf_op jit(solution)/shard_map/ppermute | solution.py:9
  46.9 12.2 %collective-permute-start.8 = (bf16[2,128,1,128]{3,1,2,0:T(8,128)(2,1)S(1)}, bf16[2,128,1,128]{3,1,2,0:T(8,128)(2,1)S(1)}, u32[]{:S(2)}, u32[]{:S(2)}) collective-permute-start(bf16[2,128,1,128]{3,1,2,0:T(8,128)(2,1)S(1)} %broadcast_select_fusion.2), channel_id=1, source_target_pairs={{0,64},{8,72},{16,80},{24,88},{32,96},{40,104},{48,112},{56,120},{... | collective-permute-start | bytes 196616 | tf_op jit(solution)/shard_map/ppermute | solution.py:9
  53.6 7.4 %collective-permute-start.4 = (bf16[2,128,1,128]{3,1,2,0:T(8,128)(2,1)S(1)}, bf16[2,128,1,128]{3,1,2,0:T(8,128)(2,1)S(1)}, u32[]{:S(2)}, u32[]{:S(2)}) collective-permute-start(bf16[2,128,1,128]{3,1,2,0:T(8,128)(2,1)S(1)} %broadcast_select_fusion.9), channel_id=1, source_target_pairs={{0,128},{8,136},{16,144},{24,152},{32,160},{40,168},{48,176},{56,1... | collective-permute-start | bytes 196616 | tf_op jit(solution)/shard_map/ppermute | solution.py:9
  59.1 8.4 %collective-permute-start.9 = (bf16[2,128,1,128]{3,1,2,0:T(8,128)(2,1)S(1)}, bf16[2,128,1,128]{3,1,2,0:T(8,128)(2,1)S(1)}, u32[]{:S(2)}, u32[]{:S(2)}) collective-permute-start(bf16[2,128,1,128]{3,1,2,0:T(8,128)(2,1)S(1)} %broadcast_select_fusion.3), channel_id=1, source_target_pairs={{0,128},{8,136},{16,144},{24,152},{32,160},{40,168},{48,176},{56,1... | collective-permute-start | bytes 196616 | tf_op jit(solution)/shard_map/ppermute | solution.py:9
  61.1 12.0 %collective-permute-start.5 = (bf16[2,128,1,128]{3,1,2,0:T(8,128)(2,1)S(1)}, bf16[2,128,1,128]{3,1,2,0:T(8,128)(2,1)S(1)}, u32[]{:S(2)}, u32[]{:S(2)}) collective-permute-start(bf16[2,128,1,128]{3,1,2,0:T(8,128)(2,1)S(1)} %broadcast_select_fusion.10), channel_id=1, source_target_pairs={{0,256},{8,264},{16,272},{24,280},{32,288},{40,296},{48,304},{56,3... | collective-permute-start | bytes 196616 | tf_op jit(solution)/shard_map/ppermute | solution.py:9
  67.6 8.6 %collective-permute-start.10 = (bf16[2,128,1,128]{3,1,2,0:T(8,128)(2,1)S(1)}, bf16[2,128,1,128]{3,1,2,0:T(8,128)(2,1)S(1)}, u32[]{:S(2)}, u32[]{:S(2)}) collective-permute-start(bf16[2,128,1,128]{3,1,2,0:T(8,128)(2,1)S(1)} %broadcast_select_fusion.4), channel_id=1, source_target_pairs={{0,256},{8,264},{16,272},{24,280},{32,288},{40,296},{48,304},{56,3... | collective-permute-start | bytes 196616 | tf_op jit(solution)/shard_map/ppermute | solution.py:9
Sparse Core Ops, SparseCore 0:
  9.5 135.8 all-gather.1
  154.7 107.2 reduce-scatter.1
where the time goes:
time: 271 us; the launch traced here: 270 us
  waiting for transfers between devices  194 us (72%)
  starting transfers between devices  34.8 us (13%)
  between operations  22.3 us (8%)
  matrix products  12.2 us (5%)
  other arithmetic  3.94 us (1%)
  local copies, waits for them, and re-layouts  2.74 us (1%)
    reduce_scatter x1, waiting for transfers between devices, per_device(): lax.psum_scatter(partial_terms, 'head', scatter_dimension=1, tiled=True)  107 us
    all_gather x1, waiting for transfers between devices, per_device(): lax.all_gather(out_weight, 'seq', axis=1, tiled=True)  66.9 us
    ppermute x11, starting transfers between devices, from_partner(): lax.ppermute(shard, axis, [(i, i ^ 1 << distance) for i in range(lax.axis...  34.8 us
    ppermute x11, waiting for transfers between devices, from_partner(): lax.ppermute(shard, axis, [(i, i ^ 1 << distance) for i in range(lax.axis...  19.4 us
    dot_general x1, matrix products, per_device(): jnp.dot(flat_rows, lax.all_gather(out_weight, 'seq', axis=1, tiled=True),...  9.14 us
  transfers between devices with their start and end apart: 13, of which 10 were waited for; matrix products, arithmetic and copies ran while one was open for 3% of the time, Pallas kernels for 0%

commit v1 on v0

--- a/solution.py
+++ b/solution.py
@@ -3,6 +3,13 @@
 import jax.numpy as jnp
 from jax import lax
 from jax.sharding import PartitionSpec as P
+
+
+def all_by_exchange(x, axis, along):
+    size = lax.axis_size(axis)
+    blocks = jnp.stack([x for _ in range(size)])
+    blocks = lax.all_to_all(blocks, axis, split_axis=0, concat_axis=0)
+    return jnp.concatenate(blocks, axis=along)
 
 
 def from_partner(shard, axis, distance):
@@ -87,9 +94,7 @@
     attended = (weighted / jnp.moveaxis(row_total, 2, 0)[..., None]).astype(jnp.bfloat16)
     flat_rows = attended.reshape(all_rows, local_kv * group_size * head_dim)
     partial_terms = jnp.dot(
-        flat_rows,
-        lax.all_gather(out_weight, "seq", axis=1, tiled=True),
-        preferred_element_type=jnp.float32,
+        flat_rows, all_by_exchange(out_weight, "seq", 1), preferred_element_type=jnp.float32
     )
     return lax.psum_scatter(partial_terms, "head", scatter_dimension=1, tiled=True).astype(
         jnp.bfloat16

time: 271 us -> 450 us (1.66)
  waiting for transfers between devices: 194 us -> 345 us
  starting transfers between devices: 34.8 us -> 60.2 us
  local copies, waits for them, and re-layouts: 2.74 us -> 7.49 us
    ppermute x11, waiting for transfers between devices: 19.4 us -> 235 us  [from_partner(): lax.ppermute(shard, axis, [(i, i ^ 1 << distance) for i in range(lax.axis...]
    all_gather x1 -> x0, waiting for transfers between devices: 66.9 us -> none  [per_device(): lax.all_gather(out_weight, 'seq', axis=1, tiled=True)]
    all_to_all x0 -> x1, starting transfers between devices: none -> 13.8 us  [all_by_exchange(): blocks = lax.all_to_all(blocks, axis, split_axis=0, concat_axis=0)]
    ppermute x11, starting transfers between devices: 34.8 us -> 46.3 us  [from_partner(): lax.ppermute(shard, axis, [(i, i ^ 1 << distance) for i in range(lax.axis...]
    another operation x0 -> x1, local copies, waits for them, and re-layouts: none -> 6.12 us  [all_by_exchange(): blocks = jnp.stack([x for _ in range(size)])]
  transfers between devices with their start and end apart: 13 -> 13, of which waited for: 10 -> 8; matrix products, arithmetic and copies ran while one was open for 3% -> 1% of each run, Pallas kernels for 0% -> 0%
where the time goes in v1:
time: 450 us; the launch traced here: 449 us
  waiting for transfers between devices  345 us (77%)
  starting transfers between devices  60.2 us (13%)
  between operations  22.9 us (5%)
  matrix products  10.6 us (2%)
  local copies, waits for them, and re-layouts  7.49 us (2%)
    ppermute x11, waiting for transfers between devices, from_partner(): lax.ppermute(shard, axis, [(i, i ^ 1 << distance) for i in range(lax.axis...  235 us
    reduce_scatter x1, waiting for transfers between devices, per_device(): lax.psum_scatter(partial_terms, 'head', scatter_dimension=1, tiled=True)  110 us
    ppermute x11, starting transfers between devices, from_partner(): lax.ppermute(shard, axis, [(i, i ^ 1 << distance) for i in range(lax.axis...  46.3 us
    all_to_all x1, starting transfers between devices, all_by_exchange(): blocks = lax.all_to_all(blocks, axis, split_axis=0, concat_axis=0)  13.8 us
    dot_general x1, matrix products, per_device(): jnp.dot(flat_rows, all_by_exchange(out_weight, 'seq', 1), preferred_eleme...  9.15 us
  transfers between devices with their start and end apart: 13, of which 8 were waited for; matrix products, arithmetic and copies ran while one was open for 1% of the time, Pallas kernels for 0%

profile of v1, /device:TPU:8, one launch (start us, length us, event | category | flops | bytes accessed | tf_op | source)
XLA Modules:
  0.0 448.8 jit_solution(10436931591715507929)
XLA Ops:
  6.5 6.1 %stack.11 = bf16[64,1024,80]{1,2,0:T(8,128)(2,1)} broadcast(bf16[1024,80]{0,1:T(8,128)(2,1)} %param.11), dimensions={1,2} | broadcast | bytes 10649600 | tf_op jit(solution)/shard_map/stack | solution.py:10
  12.7 13.8 %all-to-all-start = ((bf16[64,1024,80]{1,2,0:T(8,128)(2,1)}), bf16[64,1024,80]{1,2,0:T(8,128)(2,1)}, u32[]{:S(2)}, u32[]{:S(2)}) async-start(bf16[64,1024,80]{1,2,0:T(8,128)(2,1)} %stack.11), calls=%async_computation | async-start | bytes 20971520 | tf_op jit(solution)/shard_map/all_to_all | solution.py:11
  26.6 2.1 collective-permute-start
  28.7 0.7 constant_dynamic-slice_fusion.1
  33.4 0.7 fusion.31
  39.6 2.3 collective-permute-start.1
  41.9 0.2 fusion.33
  42.2 3.6 collective-permute-start.6
  45.8 226.4 %collective-permute-done.1 = bf16[2,128,1,128]{3,1,2,0:T(8,128)(2,1)S(1)} collective-permute-done((bf16[2,128,1,128]{3,1,2,0:T(8,128)(2,1)S(1)}, bf16[2,128,1,128]{3,1,2,0:T(8,128)(2,1)S(1)}, u32[]{:S(2)}, u32[]{:S(2)}) %collective-permute-start.1) | collective-permute-done | bytes 65568 | tf_op jit(solution)/shard_map/ppermute | solution.py:16
  272.1 9.8 %collective-permute-start.2 = (bf16[2,128,1,128]{3,1,2,0:T(8,128)(2,1)S(1)}, bf16[2,128,1,128]{3,1,2,0:T(8,128)(2,1)S(1)}, u32[]{:S(2)}, u32[]{:S(2)}) collective-permute-start(bf16[2,128,1,128]{3,1,2,0:T(8,128)(2,1)S(1)} %broadcast_select_fusion.7), channel_id=1, source_target_pairs={{0,32},{8,40},{16,48},{24,56},{32,0},{40,8},{48,16},{56,24},{64,96... | collective-permute-start | bytes 196616 | tf_op jit(solution)/shard_map/ppermute | solution.py:16
  282.0 1.9 collective-permute-start.7
  283.9 1.9 collective-permute-done.2
  285.8 1.9 collective-permute-start.3
  287.7 1.3 collective-permute-done.7
  289.0 6.6 %collective-permute-start.8 = (bf16[2,128,1,128]{3,1,2,0:T(8,128)(2,1)S(1)}, bf16[2,128,1,128]{3,1,2,0:T(8,128)(2,1)S(1)}, u32[]{:S(2)}, u32[]{:S(2)}) collective-permute-start(bf16[2,128,1,128]{3,1,2,0:T(8,128)(2,1)S(1)} %broadcast_select_fusion.2), channel_id=1, source_target_pairs={{0,64},{8,72},{16,80},{24,88},{32,96},{40,104},{48,112},{56,120},{... | collective-permute-start | bytes 196616 | tf_op jit(solution)/shard_map/ppermute | solution.py:16
  295.6 0.3 collective-permute-done.3
  295.9 1.9 collective-permute-start.4
  297.8 1.7 collective-permute-done.8
  299.6 2.2 collective-permute-start.9
  301.8 0.5 collective-permute-done.4
  302.3 10.1 %collective-permute-start.5 = (bf16[2,128,1,128]{3,1,2,0:T(8,128)(2,1)S(1)}, bf16[2,128,1,128]{3,1,2,0:T(8,128)(2,1)S(1)}, u32[]{:S(2)}, u32[]{:S(2)}) collective-permute-start(bf16[2,128,1,128]{3,1,2,0:T(8,128)(2,1)S(1)} %broadcast_select_fusion.10), channel_id=1, source_target_pairs={{0,256},{8,264},{16,272},{24,280},{32,288},{40,296},{48,304},{56,3... | collective-permute-start | bytes 196616 | tf_op jit(solution)/shard_map/ppermute | solution.py:16
  312.5 4.0 collective-permute-start.10
  316.5 3.2 collective-permute-done.10
  319.8 0.2 fusion.32
  320.0 0.2 fusion.34
  320.3 0.2 fusion.12
  320.5 0.2 fusion.17
  320.8 0.3 convolution_bitcast_fusion
  321.1 0.3 fusion.9
  321.3 9.2 %fusion.35 = f32[128,5120]{1,0:T(8,128)} fusion(bf16[128,1024]{0,1:T(8,128)(2,1)S(1)} %bitcast.98, bf16[1024,5120]{0,1:T(8,128)(2,1)} %bitcast.39), kind=kOutput, calls=%fused_computation.73 | convolution fusion | flops 1342177280 | bytes 13369344 | tf_op jit(solution)/shard_map/dot_general | solution.py:96
  330.5 109.8 %reduce-scatter.2.cloned.1.call-done = f32[128,640]{1,0:T(8,128)} async-done(((f32[128,5120]{1,0:T(8,128)}), f32[128,640]{1,0:T(8,128)}) %reduce-scatter.2.cloned.1.call-update) | async-done | bytes 327696 | tf_op jit(solution)/shard_map/reduce_scatter | solution.py:99
  440.3 1.7 convert_element_type.19
  (38 shorter events, 0.6 us)
Async XLA Ops:
  6.5 35.4 %copy-start = (bf16[128,8,128]{2,1,0:T(8,128)(2,1)S(1)}, bf16[128,8,128]{2,1,0:T(8,128)(2,1)}, u32[]{:S(2)}) copy-start(bf16[128,8,128]{2,1,0:T(8,128)(2,1)} %param.6) | copy-start | bytes 786436
  12.7 13.9 %copy-start.1 = (bf16[128,1,128]{2,0,1:T(8,128)(2,1)S(1)}, bf16[128,1,128]{2,0,1:T(8,128)(2,1)}, u32[]{:S(2)}) copy-start(bf16[128,1,128]{2,0,1:T(8,128)(2,1)} %param.7) | copy-start | bytes 98308
  12.7 13.9 %copy-start.2 = (bf16[128,1,128]{2,0,1:T(8,128)(2,1)S(1)}, bf16[128,1,128]{2,0,1:T(8,128)(2,1)}, u32[]{:S(2)}) copy-start(bf16[128,1,128]{2,0,1:T(8,128)(2,1)} %param.8) | copy-start | bytes 98308
  12.7 16.0 %copy-start.4 = (s32[2,64]{1,0:T(2,128)S(1)}, s32[2,64]{1,0:T(2,128)}, u32[]{:S(2)}) copy-start(s32[2,64]{1,0:T(2,128)} %param.10) | copy-start | bytes 1540
  12.7 20.7 %copy-start.3 = (s32[64]{0:T(128)S(1)}, s32[64]{0:T(128)}, u32[]{:S(2)}) copy-start(s32[64]{0:T(128)} %param.9) | copy-start | bytes 772
  12.7 308.7 %all-to-all-start = ((bf16[64,1024,80]{1,2,0:T(8,128)(2,1)}), bf16[64,1024,80]{1,2,0:T(8,128)(2,1)}, u32[]{:S(2)}, u32[]{:S(2)}) async-start(bf16[64,1024,80]{1,2,0:T(8,128)(2,1)} %stack.11), calls=%async_computation | async-start | bytes 20971520 | tf_op jit(solution)/shard_map/all_to_all | solution.py:11
  26.5 413.8 %reduce-scatter.2.cloned.1.call-start = ((), (), s32[]{:S(2)}) async-start(), calls=%async_computation.2 | async-start | bytes 2949120 | tf_op jit(solution)/shard_map/reduce_scatter | solution.py:99
  26.6 13.0 %collective-permute-start = (bf16[2,128,1,128]{3,1,2,0:T(8,128)(2,1)S(1)}, bf16[2,128,1,128]{3,1,2,0:T(8,128)(2,1)S(1)}, u32[]{:S(2)}, u32[]{:S(2)}) collective-permute-start(bf16[2,128,1,128]{3,1,2,0:T(8,128)(2,1)S(1)} %pad_maximum_fusion), channel_id=1, source_target_pairs={{0,8},{8,0},{16,24},{24,16},{32,40},{40,32},{48,56},{56,48},{64,72... | collective-permute-start | bytes 196616 | tf_op jit(solution)/shard_map/ppermute | solution.py:16
  39.6 232.5 %collective-permute-start.1 = (bf16[2,128,1,128]{3,1,2,0:T(8,128)(2,1)S(1)}, bf16[2,128,1,128]{3,1,2,0:T(8,128)(2,1)S(1)}, u32[]{:S(2)}, u32[]{:S(2)}) collective-permute-start(bf16[2,128,1,128]{3,1,2,0:T(8,128)(2,1)S(1)} %get-tuple-element.8), channel_id=1, source_target_pairs={{0,16},{8,24},{16,0},{24,8},{32,48},{40,56},{48,32},{56,40},{64,80... | collective-permute-start | bytes 196616 | tf_op jit(solution)/shard_map/ppermute | solution.py:16
  42.2 239.7 %collective-permute-start.6 = (bf16[2,128,1,128]{3,1,2,0:T(8,128)(2,1)S(1)}, bf16[2,128,1,128]{3,1,2,0:T(8,128)(2,1)S(1)}, u32[]{:S(2)}, u32[]{:S(2)}) collective-permute-start(bf16[2,128,1,128]{3,1,2,0:T(8,128)(2,1)S(1)} %get-tuple-element.9), channel_id=1, source_target_pairs={{0,16},{8,24},{16,0},{24,8},{32,48},{40,56},{48,32},{56,40},{64,80... | collective-permute-start | bytes 196616 | tf_op jit(solution)/shard_map/ppermute | solution.py:16
  272.1 13.6 %collective-permute-start.2 = (bf16[2,128,1,128]{3,1,2,0:T(8,128)(2,1)S(1)}, bf16[2,128,1,128]{3,1,2,0:T(8,128)(2,1)S(1)}, u32[]{:S(2)}, u32[]{:S(2)}) collective-permute-start(bf16[2,128,1,128]{3,1,2,0:T(8,128)(2,1)S(1)} %broadcast_select_fusion.7), channel_id=1, source_target_pairs={{0,32},{8,40},{16,48},{24,56},{32,0},{40,8},{48,16},{56,24},{64,96... | collective-permute-start | bytes 196616 | tf_op jit(solution)/shard_map/ppermute | solution.py:16
  282.0 7.1 %collective-permute-start.7 = (bf16[2,128,1,128]{3,1,2,0:T(8,128)(2,1)S(1)}, bf16[2,128,1,128]{3,1,2,0:T(8,128)(2,1)S(1)}, u32[]{:S(2)}, u32[]{:S(2)}) collective-permute-start(bf16[2,128,1,128]{3,1,2,0:T(8,128)(2,1)S(1)} %broadcast_select_fusion.1), channel_id=1, source_target_pairs={{0,32},{8,40},{16,48},{24,56},{32,0},{40,8},{48,16},{56,24},{64,96... | collective-permute-start | bytes 196616 | tf_op jit(solution)/shard_map/ppermute | solution.py:16
  285.8 10.1 %collective-permute-start.3 = (bf16[2,128,1,128]{3,1,2,0:T(8,128)(2,1)S(1)}, bf16[2,128,1,128]{3,1,2,0:T(8,128)(2,1)S(1)}, u32[]{:S(2)}, u32[]{:S(2)}) collective-permute-start(bf16[2,128,1,128]{3,1,2,0:T(8,128)(2,1)S(1)} %broadcast_select_fusion.8), channel_id=1, source_target_pairs={{0,64},{8,72},{16,80},{24,88},{32,96},{40,104},{48,112},{56,120},{... | collective-permute-start | bytes 196616 | tf_op jit(solution)/shard_map/ppermute | solution.py:16
  289.0 10.5 %collective-permute-start.8 = (bf16[2,128,1,128]{3,1,2,0:T(8,128)(2,1)S(1)}, bf16[2,128,1,128]{3,1,2,0:T(8,128)(2,1)S(1)}, u32[]{:S(2)}, u32[]{:S(2)}) collective-permute-start(bf16[2,128,1,128]{3,1,2,0:T(8,128)(2,1)S(1)} %broadcast_select_fusion.2), channel_id=1, source_target_pairs={{0,64},{8,72},{16,80},{24,88},{32,96},{40,104},{48,112},{56,120},{... | collective-permute-start | bytes 196616 | tf_op jit(solution)/shard_map/ppermute | solution.py:16
  295.9 6.4 %collective-permute-start.4 = (bf16[2,128,1,128]{3,1,2,0:T(8,128)(2,1)S(1)}, bf16[2,128,1,128]{3,1,2,0:T(8,128)(2,1)S(1)}, u32[]{:S(2)}, u32[]{:S(2)}) collective-permute-start(bf16[2,128,1,128]{3,1,2,0:T(8,128)(2,1)S(1)} %broadcast_select_fusion.9), channel_id=1, source_target_pairs={{0,128},{8,136},{16,144},{24,152},{32,160},{40,168},{48,176},{56,1... | collective-permute-start | bytes 196616 | tf_op jit(solution)/shard_map/ppermute | solution.py:16
  299.6 12.9 %collective-permute-start.9 = (bf16[2,128,1,128]{3,1,2,0:T(8,128)(2,1)S(1)}, bf16[2,128,1,128]{3,1,2,0:T(8,128)(2,1)S(1)}, u32[]{:S(2)}, u32[]{:S(2)}) collective-permute-start(bf16[2,128,1,128]{3,1,2,0:T(8,128)(2,1)S(1)} %broadcast_select_fusion.3), channel_id=1, source_target_pairs={{0,128},{8,136},{16,144},{24,152},{32,160},{40,168},{48,176},{56,1... | collective-permute-start | bytes 196616 | tf_op jit(solution)/shard_map/ppermute | solution.py:16
  302.3 14.2 %collective-permute-start.5 = (bf16[2,128,1,128]{3,1,2,0:T(8,128)(2,1)S(1)}, bf16[2,128,1,128]{3,1,2,0:T(8,128)(2,1)S(1)}, u32[]{:S(2)}, u32[]{:S(2)}) collective-permute-start(bf16[2,128,1,128]{3,1,2,0:T(8,128)(2,1)S(1)} %broadcast_select_fusion.10), channel_id=1, source_target_pairs={{0,256},{8,264},{16,272},{24,280},{32,288},{40,296},{48,304},{56,3... | collective-permute-start | bytes 196616 | tf_op jit(solution)/shard_map/ppermute | solution.py:16
  312.5 7.3 %collective-permute-start.10 = (bf16[2,128,1,128]{3,1,2,0:T(8,128)(2,1)S(1)}, bf16[2,128,1,128]{3,1,2,0:T(8,128)(2,1)S(1)}, u32[]{:S(2)}, u32[]{:S(2)}) collective-permute-start(bf16[2,128,1,128]{3,1,2,0:T(8,128)(2,1)S(1)} %broadcast_select_fusion.4), channel_id=1, source_target_pairs={{0,256},{8,264},{16,272},{24,280},{32,288},{40,296},{48,304},{56,3... | collective-permute-start | bytes 196616 | tf_op jit(solution)/shard_map/ppermute | solution.py:16
Sparse Core Ops, SparseCore 0:
  330.6 109.6 reduce-scatter.1
